TPU v7x, 32 devices: a whole 2x2x4 slice. The times are simulated.
32 devices in a mesh: fsdp: 8 (over z, core), mp: 4 (over y, x).
Axes of the slice: x: 2, y: 2, z: 4, core: 2. Of those that a mesh axis runs over, the one named last changes fastest.
Arguments:
- inputs: bfloat16 [2048, 2048], P('fsdp'), may hold values from -6 to 6
- cotangent: bfloat16 [2048, 2048], P('fsdp'), may hold values from -6 to 6
- lengths: int32 [2], replicated, may hold values from 256 to 1024, as said below
- attn_scale: float32 [2048], P('fsdp'), may hold values from 0.5 to 1.5
- w_query: float32 [2048, 2048], P('fsdp', 'mp'), may hold values from -0.015625 to 0.015625
- w_key: float32 [2048, 2048], P('fsdp', 'mp'), may hold values from -0.125 to 0.125
- w_value: float32 [2048, 2048], P('fsdp', 'mp'), may hold values from -0.125 to 0.125
- w_out: float32 [2048, 2048], P('mp', 'fsdp'), may hold values from -3 to 3
- rel_table: float32 [32, 32], P('fsdp', 'mp'), may hold values from -4 to 4
- ffn_scale: float32 [2048], P('fsdp'), may hold values from 0.5 to 1.5
- w_gate: float32 [2048, 5120], P('fsdp', 'mp'), may hold values from -0.125 to 0.125
- w_up: float32 [2048, 5120], P('fsdp', 'mp'), may hold values from -0.125 to 0.125
- w_down: float32 [5120, 2048], P('mp', 'fsdp'), may hold values from -0.078125 to 0.078125
Outputs:
- outputs: bfloat16 [2048, 2048], P('fsdp')
- d_inputs: bfloat16 [2048, 2048], P('fsdp')
- d_attn_scale: float32 [2048], P('fsdp')
- d_w_query: float32 [2048, 2048], P('fsdp', 'mp')
- d_w_key: float32 [2048, 2048], P('fsdp', 'mp')
- d_w_value: float32 [2048, 2048], P('fsdp', 'mp')
- d_w_out: float32 [2048, 2048], P('mp', 'fsdp')
- d_rel_table: float32 [32, 32], P('fsdp', 'mp')
- d_ffn_scale: float32 [2048], P('fsdp')
- d_w_gate: float32 [2048, 5120], P('fsdp', 'mp')
- d_w_up: float32 [2048, 5120], P('fsdp', 'mp')
- d_w_down: float32 [5120, 2048], P('mp', 'fsdp')
Inputs may be any that keep to these rules, and one draw needn't show every extreme that they name: lengths[s] slots at the start of sequence s are used, the rest is padding; in every draw some sequence is full.
All inputs are finite; a program needn't handle non-finite values.
Results may differ from a plain program's by a relative error of at most 0.019.
Values may be sent and summed in bfloat16 or wider, within the bound.
No kernel may reach another device: no remote copies, remote signals or barrier semaphores. Data moves between devices by JAX's collectives and lax.ppermute only.
A program may use at most 192 MiB of HBM per device.

v0:
```python
import jax
import jax.numpy as jnp
from jax import lax
from jax.sharding import PartitionSpec as P

GROUP = 4


THRESHOLDS = (12, 16, 23, 32, 46, 64, 91)
EPSILON = 1e-06
MASKED = -1e30


def shifted(block, axis, distance):
    devices = range(lax.axis_size(axis))
    route = [(i - distance, i) for i in devices if i - distance in devices]
    return lax.ppermute(block, axis, route)


def bucket_of(rel_offset):
    distance = jnp.abs(rel_offset)
    far_bucket = 8 + sum(((distance >= threshold).astype(jnp.int32) for threshold in THRESHOLDS))
    bucket_abs = jnp.where(distance < 8, distance, far_bucket)
    return bucket_abs + jnp.where(rel_offset > 0, 16, 0)


def bucket_onehot(first_query, query_count, key_count, bucket_count):
    span_width = query_count + key_count
    rel_offset = lax.iota(jnp.int32, span_width) - (first_query + query_count - 1)
    return (bucket_of(rel_offset)[:, None] == lax.iota(jnp.int32, bucket_count)[None, :]).astype(
        jnp.float32
    )


def offset_bias(table_f32, first_query, query_count, key_count):
    span_width = query_count + key_count
    one_hot = bucket_onehot(first_query, query_count, key_count, table_f32.shape[0])
    bias_line = jnp.dot(one_hot, table_f32, precision=lax.Precision.HIGHEST).T
    repeated = jnp.tile(bias_line, (1, query_count))
    skewed = lax.slice_in_dim(
        repeated, query_count - 1, query_count - 1 + query_count * (span_width - 1), axis=1
    )
    return skewed.reshape(bias_line.shape[0], query_count, span_width - 1)[:, :, :key_count]


def offset_grad(grad_scores, first_query, query_count, key_count, bucket_count):
    span_width = query_count + key_count
    head_count = grad_scores.shape[0]
    widened = jnp.pad(grad_scores, ((0, 0), (0, 0), (0, span_width - 1 - key_count)))
    flattened = jnp.pad(
        widened.reshape(head_count, query_count * (span_width - 1)), ((0, 0), (query_count - 1, 1))
    )
    summed = jnp.sum(flattened.reshape(head_count, query_count, span_width), axis=1)
    one_hot = bucket_onehot(first_query, query_count, key_count, bucket_count)
    return jnp.dot(one_hot.T, summed.T, precision=lax.Precision.HIGHEST)


def contract_rows(left, right):
    return lax.dot_general(
        left, right, (((0,), (0,)), ((), ())), preferred_element_type=jnp.float32
    )


def contract_cols(left, right):
    return lax.dot_general(
        left, right, (((1,), (1,)), ((), ())), preferred_element_type=jnp.float32
    )


def gelu_tanh(values):
    return jax.nn.gelu(values, approximate=True)


def group_collect(keys_local, values_local, member, tok_rows):
    key_pieces = []
    value_pieces = []
    for distance in range(GROUP - 1, -GROUP, -1):
        if distance == 0:
            key_pieces.append(keys_local)
            value_pieces.append(values_local)
        else:
            moved_keys, moved_values = shifted((keys_local, values_local), "fsdp", distance)
            key_pieces.append(moved_keys)
            value_pieces.append(moved_values)
    first_piece = GROUP - 1 - member
    keys_seq = lax.dynamic_slice_in_dim(jnp.stack(key_pieces), first_piece, GROUP, 0)
    values_seq = lax.dynamic_slice_in_dim(jnp.stack(value_pieces), first_piece, GROUP, 0)
    return (keys_seq.reshape(GROUP * tok_rows, -1), values_seq.reshape(GROUP * tok_rows, -1))


def group_return(keys_part, values_part, member, tok_rows):
    own_keys = lax.dynamic_slice_in_dim(keys_part, member * tok_rows, tok_rows, 0)
    own_values = lax.dynamic_slice_in_dim(values_part, member * tok_rows, tok_rows, 0)
    for distance in list(range(1, GROUP)) + list(range(-1, -GROUP, -1)):
        target = member + distance
        inside = (target >= 0) & (target < GROUP)
        clamped = jnp.clip(target, 0, GROUP - 1)
        send_keys = jnp.where(
            inside, lax.dynamic_slice_in_dim(keys_part, clamped * tok_rows, tok_rows, 0), 0.0
        )
        send_values = jnp.where(
            inside, lax.dynamic_slice_in_dim(values_part, clamped * tok_rows, tok_rows, 0), 0.0
        )
        got_keys, got_values = shifted((send_keys, send_values), "fsdp", distance)
        own_keys = own_keys + got_keys
        own_values = own_values + got_values
    return (own_keys, own_values)


def local(
    inputs,
    cotangent,
    lengths,
    attn_scale,
    w_query,
    w_key,
    w_value,
    w_out,
    rel_table,
    ffn_scale,
    w_gate,
    w_up,
    w_down,
):
    low_type = jnp.bfloat16
    tok_rows = inputs.shape[0]
    seq_len = tok_rows * GROUP
    block_rows = min(512, tok_rows)
    block_count = tok_rows // block_rows
    position = lax.axis_index("fsdp")
    member = position % GROUP
    sequence = position // GROUP
    length = lax.dynamic_index_in_dim(lengths, sequence, 0, keepdims=False)
    first_row = member * tok_rows
    query_valid = first_row + lax.iota(jnp.int32, tok_rows) < length
    key_valid = lax.iota(jnp.int32, seq_len) < length
    resid = inputs.astype(jnp.float32)
    gain_one, query_full, key_full, value_full, out_full, table_low = (
        lax.all_gather(attn_scale.astype(low_type), "fsdp", axis=0, tiled=True),
        lax.all_gather(w_query.astype(low_type), "fsdp", axis=0, tiled=True),
        lax.all_gather(w_key.astype(low_type), "fsdp", axis=0, tiled=True),
        lax.all_gather(w_value.astype(low_type), "fsdp", axis=0, tiled=True),
        lax.all_gather(w_out.astype(low_type), "fsdp", axis=1, tiled=True),
        lax.all_gather(rel_table.astype(low_type), "fsdp", axis=0, tiled=True),
    )
    gain_one = gain_one.astype(jnp.float32)
    table_f32 = table_low.astype(jnp.float32)
    bucket_count = table_f32.shape[0]
    head_count = table_f32.shape[1]
    inner_width = query_full.shape[1]
    head_width = inner_width // head_count
    inv_one = lax.rsqrt(jnp.mean(resid * resid, axis=1, keepdims=True) + EPSILON)
    normed_one = resid * inv_one
    hidden_one = (normed_one * gain_one).astype(low_type)
    queries = jnp.dot(hidden_one, query_full, preferred_element_type=jnp.float32).astype(low_type)
    keys_local = jnp.dot(hidden_one, key_full, preferred_element_type=jnp.float32).astype(low_type)
    values_local = jnp.dot(hidden_one, value_full, preferred_element_type=jnp.float32).astype(
        low_type
    )
    keys_seq, values_seq = group_collect(keys_local, values_local, member, tok_rows)
    query_heads = queries.reshape(tok_rows, head_count, head_width)
    key_heads = keys_seq.reshape(seq_len, head_count, head_width)
    value_heads = values_seq.reshape(seq_len, head_count, head_width)

    def scores_of(block_start):
        pos_bias = offset_bias(table_f32, first_row + block_start, block_rows, seq_len)
        raw_scores = (
            jnp.einsum("qhd,khd->hqk", query_heads, key_heads, preferred_element_type=jnp.float32)
            + pos_bias
        )
        return (query_heads, jnp.where(key_valid[None, None, :], raw_scores, MASKED))

    def forward_block(block_index):
        query_block, raw_scores = scores_of(block_index * block_rows)
        row_max = jnp.max(raw_scores, axis=2, keepdims=True)
        exp_scores = jnp.exp(raw_scores - row_max)
        row_total = jnp.sum(exp_scores, axis=2, keepdims=True)
        attn_prob = (exp_scores / row_total).astype(low_type)
        block_out = jnp.einsum(
            "hqk,khd->qhd", attn_prob, value_heads, preferred_element_type=jnp.float32
        ).astype(low_type)
        return (block_out, row_max[:, :, 0] + jnp.log(row_total[:, :, 0]))

    attended, log_total = lax.map(forward_block, lax.iota(jnp.int32, block_count))
    attended = attended.reshape(tok_rows, inner_width)
    gain_two, gate_full, up_full, down_full = (
        lax.all_gather(ffn_scale.astype(low_type), "fsdp", axis=0, tiled=True),
        lax.all_gather(w_gate.astype(low_type), "fsdp", axis=0, tiled=True),
        lax.all_gather(w_up.astype(low_type), "fsdp", axis=0, tiled=True),
        lax.all_gather(w_down.astype(low_type), "fsdp", axis=1, tiled=True),
    )
    gain_two = gain_two.astype(jnp.float32)
    mixed_attn = lax.psum(jnp.dot(attended, out_full, preferred_element_type=jnp.float32), "mp")
    after_attn = resid + mixed_attn
    inv_two = lax.rsqrt(jnp.mean(after_attn * after_attn, axis=1, keepdims=True) + EPSILON)
    normed_two = after_attn * inv_two
    hidden_rows = (normed_two * gain_two).astype(low_type)
    gate_pre = jnp.dot(hidden_rows, gate_full, preferred_element_type=jnp.float32)
    up_pre = jnp.dot(hidden_rows, up_full, preferred_element_type=jnp.float32)
    gelu_value, gelu_pull = jax.vjp(gelu_tanh, gate_pre)
    hidden_act = (gelu_value * up_pre).astype(low_type)
    mixed_ffn = lax.psum(
        jnp.dot(hidden_act, down_full, preferred_element_type=jnp.float32).astype(jnp.bfloat16),
        "mp",
    ).astype(jnp.float32)
    after_ffn = after_attn + mixed_ffn
    layer_out = jnp.where(query_valid[:, None], after_ffn, 0.0).astype(low_type)
    grad_two = jnp.where(query_valid[:, None], cotangent.astype(jnp.float32), 0.0)
    grad_two_low = grad_two.astype(low_type)
    d_down = contract_rows(hidden_act, grad_two_low)
    d_hidden = contract_cols(grad_two_low, down_full)
    (d_gate_pre,) = gelu_pull(d_hidden * up_pre)
    d_gate_low = d_gate_pre.astype(low_type)
    d_up_low = (d_hidden * gelu_value).astype(low_type)
    d_gate_w = contract_rows(hidden_rows, d_gate_low)
    d_up_w = contract_rows(hidden_rows, d_up_low)
    d_norm_two = lax.psum(
        contract_cols(d_gate_low, gate_full) + contract_cols(d_up_low, up_full), "mp"
    )
    d_gain_two = jnp.sum(d_norm_two * normed_two, axis=0)
    ffn_grads = (
        lax.psum_scatter(d_gain_two, "fsdp", scatter_dimension=0, tiled=True),
        lax.psum_scatter(d_gate_w, "fsdp", scatter_dimension=0, tiled=True),
        lax.psum_scatter(d_up_w, "fsdp", scatter_dimension=0, tiled=True),
        lax.psum_scatter(d_down, "fsdp", scatter_dimension=1, tiled=True),
    )
    inner_two = d_norm_two * gain_two
    grad_one = grad_two + inv_two * (
        inner_two - normed_two * jnp.mean(inner_two * normed_two, axis=1, keepdims=True)
    )
    grad_one_rows_low = grad_one.astype(low_type)
    d_out_w = contract_rows(attended, grad_one_rows_low)
    d_attended = contract_cols(grad_one_rows_low, out_full).astype(low_type)
    d_out_heads = d_attended.reshape(tok_rows, head_count, head_width)

    def backward_block(carry, block_index):
        d_keys, d_values, d_table = carry
        block_start = block_index * block_rows
        query_block, raw_scores = scores_of(block_start)
        block_lse = lax.dynamic_index_in_dim(log_total, block_index, 0, keepdims=False)
        attn_prob = jnp.exp(raw_scores - block_lse[:, :, None])
        d_prob = jnp.einsum(
            "qhd,khd->hqk", d_out_heads, value_heads, preferred_element_type=jnp.float32
        )
        d_scores = (
            attn_prob * (d_prob - jnp.sum(attn_prob * d_prob, axis=2, keepdims=True))
        ).astype(low_type)
        d_query_block = jnp.einsum(
            "hqk,khd->qhd", d_scores, key_heads, preferred_element_type=jnp.float32
        ).astype(low_type)
        d_keys = d_keys + jnp.einsum(
            "hqk,qhd->khd", d_scores, query_block, preferred_element_type=jnp.float32
        )
        d_values = d_values + jnp.einsum(
            "hqk,qhd->khd",
            attn_prob.astype(low_type),
            d_out_heads,
            preferred_element_type=jnp.float32,
        )
        d_table = d_table + offset_grad(
            d_scores.astype(jnp.float32), first_row + block_start, block_rows, seq_len, bucket_count
        )
        return ((d_keys, d_values, d_table), d_query_block)

    zero_keys = jnp.zeros((seq_len, head_count, head_width), jnp.float32)
    zero_table = jnp.zeros((bucket_count, head_count), jnp.float32)
    (d_keys_seq, d_values_seq, d_table), d_query_blocks = lax.scan(
        backward_block, (zero_keys, zero_keys, zero_table), lax.iota(jnp.int32, block_count)
    )
    d_queries_low = d_query_blocks.reshape(tok_rows, inner_width)
    d_keys_seq = d_keys_seq.reshape(seq_len, inner_width)
    d_values_seq = d_values_seq.reshape(seq_len, inner_width)
    mine_keys, mine_values = group_return(d_keys_seq, d_values_seq, member, tok_rows)
    d_keys_low = mine_keys.astype(low_type)
    d_values_low = mine_values.astype(low_type)
    d_query_w = contract_rows(hidden_one, d_queries_low)
    d_key_w = contract_rows(hidden_one, d_keys_low)
    d_value_w = contract_rows(hidden_one, d_values_low)
    norm_part = (
        contract_cols(d_queries_low, query_full)
        + contract_cols(d_keys_low, key_full)
        + contract_cols(d_values_low, value_full)
    )
    d_norm_one = lax.psum(norm_part, "mp")
    d_gain_one = jnp.sum(d_norm_one * normed_one, axis=0)
    attn_grads = (
        lax.psum_scatter(d_gain_one, "fsdp", scatter_dimension=0, tiled=True),
        lax.psum_scatter(d_query_w, "fsdp", scatter_dimension=0, tiled=True),
        lax.psum_scatter(d_key_w, "fsdp", scatter_dimension=0, tiled=True),
        lax.psum_scatter(d_value_w, "fsdp", scatter_dimension=0, tiled=True),
        lax.psum_scatter(d_out_w, "fsdp", scatter_dimension=1, tiled=True),
        lax.psum_scatter(d_table, "fsdp", scatter_dimension=0, tiled=True),
    )
    inner_one = d_norm_one * gain_one
    grad_input = grad_one + inv_one * (
        inner_one - normed_one * jnp.mean(inner_one * normed_one, axis=1, keepdims=True)
    )
    grad_input_low = grad_input.astype(low_type)
    return (
        layer_out,
        grad_input_low,
        attn_grads[0],
        attn_grads[1],
        attn_grads[2],
        attn_grads[3],
        attn_grads[4],
        attn_grads[5],
        ffn_grads[0],
        ffn_grads[1],
        ffn_grads[2],
        ffn_grads[3],
    )


def solution(mesh):
    in_specs = (
        P("fsdp", None),
        P("fsdp", None),
        P(),
        P("fsdp"),
        P("fsdp", "mp"),
        P("fsdp", "mp"),
        P("fsdp", "mp"),
        P("mp", "fsdp"),
        P("fsdp", "mp"),
        P("fsdp"),
        P("fsdp", "mp"),
        P("fsdp", "mp"),
        P("mp", "fsdp"),
    )
    out_specs = (
        P("fsdp", None),
        P("fsdp", None),
        P("fsdp"),
        P("fsdp", "mp"),
        P("fsdp", "mp"),
        P("fsdp", "mp"),
        P("mp", "fsdp"),
        P("fsdp", "mp"),
        P("fsdp"),
        P("fsdp", "mp"),
        P("fsdp", "mp"),
        P("mp", "fsdp"),
    )
    return jax.shard_map(local, mesh=mesh, in_specs=in_specs, out_specs=out_specs, check_vma=False)
```

profile of v0, /device:TPU:0, one launch (start us, length us, event | category | flops | bytes accessed | tf_op | source)
XLA Modules:
  0.0 1290.1 jit_solution(14534975958745252116)
XLA Ops:
  12.8 13.5 %all-gather = bf16[8,1,256]{2,1,0:T(2,128)(2,1)S(1)} all-gather(bf16[1,1,256]{2,1,0:T(2,128)(2,1)S(1)} %reshape.151), channel_id=1, replica_groups=mesh['fsdp'=8,'mp'=4] {'fsdp'}, dimensions={0}, use_global_device_ids=true | all-gather | bytes 4608 | tf_op jit(solution)/shard_map/all_gather | solution.py:139
  50.7 20.7 %reshape.140 = f32[8,256,1279]{2,1,0:T(8,128)} reshape(f32[2619392]{0:T(1024)} %reshape.162) | data formatting | bytes 20955136 | tf_op jit(solution)/shard_map/while/body/eval_jaxpr/reshape | solution.py:43
  88.2 23.7 %all-gather.13.cloned.1.call-done = bf16[2048,512]{1,0:T(8,128)(2,1)} async-done(((bf16[256,512]{1,0:T(8,128)(2,1)}), bf16[2048,512]{1,0:T(8,128)(2,1)}) %all-gather.13.cloned.1.call-update) | async-done | bytes 2097168 | tf_op jit(solution)/shard_map/all_gather | solution.py:140
  146.2 17.2 %collective-permute-done.4 = bf16[256,512]{1,0:T(8,128)(2,1)S(1)} collective-permute-done((bf16[256,512]{1,0:T(8,128)(2,1)S(1)}, bf16[256,512]{1,0:T(8,128)(2,1)S(1)}, u32[]{:S(2)}, u32[]{:S(2)}) %collective-permute-start.4) | collective-permute-done | bytes 262176 | tf_op jit(solution)/shard_map/ppermute | solution.py:17
  194.5 16.0 %all-gather.2 = bf16[8,1,256]{2,1,0:T(2,128)(2,1)S(1)} all-gather(bf16[1,1,256]{2,1,0:T(2,128)(2,1)S(1)} %reshape.155), channel_id=1, replica_groups=mesh['fsdp'=8,'mp'=4] {'fsdp'}, dimensions={0}, use_global_device_ids=true | all-gather | bytes 4608 | tf_op jit(solution)/shard_map/all_gather | solution.py:187
  211.1 52.6 %all-reduce.11.cloned.1.call-done = f32[256,2048]{1,0:T(8,128)} async-done(((f32[256,2048]{1,0:T(8,128)}), f32[256,2048]{1,0:T(8,128)}) %all-reduce.11.cloned.1.call-update) | async-done | bytes 2097168 | tf_op jit(solution)/shard_map/psum | solution.py:193
  267.1 54.9 %all-gather.19.cloned.1.call-done = bf16[2048,1280]{1,0:T(8,128)(2,1)} async-done(((bf16[256,1280]{1,0:T(8,128)(2,1)}), bf16[2048,1280]{1,0:T(8,128)(2,1)}) %all-gather.19.cloned.1.call-update) | async-done | bytes 5242896 | tf_op jit(solution)/shard_map/all_gather | solution.py:188
  327.3 51.8 %all-gather.21.cloned.1.call-done = bf16[2048,1280]{1,0:T(8,128)(2,1)} async-done(((bf16[256,1280]{1,0:T(8,128)(2,1)}), bf16[2048,1280]{1,0:T(8,128)(2,1)}) %all-gather.21.cloned.1.call-update) | async-done | bytes 5242896 | tf_op jit(solution)/shard_map/all_gather | solution.py:189
  384.5 51.6 %all-gather.23.cloned.1.call-done = bf16[1280,2048]{1,0:T(8,128)(2,1)} async-done(((bf16[1280,256]{1,0:T(8,128)(2,1)}), bf16[1280,2048]{1,0:T(8,128)(2,1)}) %all-gather.23.cloned.1.call-update) | async-done | bytes 5242896 | tf_op jit(solution)/shard_map/all_gather | solution.py:190
  454.5 62.4 %all-reduce.15.cloned.1.call-done = f32[256,2048]{1,0:T(8,128)} async-done(((f32[256,2048]{1,0:T(8,128)}), f32[256,2048]{1,0:T(8,128)}) %all-reduce.15.cloned.1.call-update) | async-done | bytes 2097168 | tf_op jit(solution)/shard_map/psum | solution.py:217
  519.1 53.9 %all-reduce.13.cloned.1.call-done = bf16[256,2048]{1,0:T(8,128)(2,1)} async-done(((bf16[256,2048]{1,0:T(8,128)(2,1)}), bf16[256,2048]{1,0:T(8,128)(2,1)}) %all-reduce.13.cloned.1.call-update) | async-done | bytes 1048592 | tf_op jit(solution)/shard_map/psum | solution.py:202
  622.4 14.0 %collective-permute-start.20 = (f32[256,512]{0,1:T(8,128)S(1)}, f32[256,512]{0,1:T(8,128)S(1)}, u32[]{:S(2)}, u32[]{:S(2)}) collective-permute-start(f32[256,512]{0,1:T(8,128)S(1)} %get-tuple-element.96), channel_id=1, source_target_pairs={{0,12},{4,16},{8,20},{12,24},{16,28},{1,13},{5,17},{9,21},{13,25},... | collective-permute-start | bytes 1572872 | tf_op jit(solution)/shard_map/ppermute | solution.py:17
  640.2 9.0 collective-permute-start.18
  705.5 11.6 reshape.164
  717.1 10.4 reshape.146
  733.5 11.1 all-reduce.17.cloned.1.call-done
  746.8 30.1 %all-reduce.5 = (f32[2048]{0:T(1024)S(1)}, f32[32,8]{1,0:T(8,128)S(1)}, f32[2048]{0:T(1024)S(1)}) all-reduce(f32[2048]{0:T(1024)S(1)} %get-tuple-element.67, f32[32,8]{1,0:T(8,128)S(1)} %fusion.36, f32[2048]{0:T(1024)S(1)} %get-tuple-element.65), channel_id=2, replica_groups=mesh['fsdp'=8,'mp'=4] {'fsdp'}, use_global_device_ids=true, to_apply=%region_12.13.clone | all-reduce | flops 4352 | bytes 34816
  781.9 16.0 %reduce-scatter.8.cloned.1.call-done = f32[256,512]{1,0:T(8,128)} async-done(((f32[2048,512]{1,0:T(8,128)}), f32[256,512]{1,0:T(8,128)}) %reduce-scatter.8.cloned.1.call-update) | async-done | bytes 524304 | tf_op jit(solution)/shard_map/reduce_scatter | solution.py:288
  797.9 51.1 %reduce-scatter.14.cloned.1.call-done = f32[512,256]{1,0:T(8,128)} async-done(((f32[512,2048]{1,0:T(8,128)}), f32[512,256]{1,0:T(8,128)}) %reduce-scatter.14.cloned.1.call-update) | async-done | bytes 524304 | tf_op jit(solution)/shard_map/reduce_scatter | solution.py:291
  849.1 51.0 %reduce-scatter.10.cloned.1.call-done = f32[256,512]{1,0:T(8,128)} async-done(((f32[2048,512]{1,0:T(8,128)}), f32[256,512]{1,0:T(8,128)}) %reduce-scatter.10.cloned.1.call-update) | async-done | bytes 524304 | tf_op jit(solution)/shard_map/reduce_scatter | solution.py:289
  900.1 51.0 %reduce-scatter.12.cloned.1.call-done = f32[256,512]{1,0:T(8,128)} async-done(((f32[2048,512]{1,0:T(8,128)}), f32[256,512]{1,0:T(8,128)}) %reduce-scatter.12.cloned.1.call-update) | async-done | bytes 524304 | tf_op jit(solution)/shard_map/reduce_scatter | solution.py:290
  951.1 110.4 %reduce-scatter.16.cloned.1.call-done = f32[256,1280]{1,0:T(8,128)} async-done(((f32[2048,1280]{1,0:T(8,128)}), f32[256,1280]{1,0:T(8,128)}) %reduce-scatter.16.cloned.1.call-update) | async-done | bytes 1310736 | tf_op jit(solution)/shard_map/reduce_scatter | solution.py:223
  1061.5 110.6 %reduce-scatter.18.cloned.1.call-done = f32[256,1280]{1,0:T(8,128)} async-done(((f32[2048,1280]{1,0:T(8,128)}), f32[256,1280]{1,0:T(8,128)}) %reduce-scatter.18.cloned.1.call-update) | async-done | bytes 1310736 | tf_op jit(solution)/shard_map/reduce_scatter | solution.py:224
  1172.2 110.6 %reduce-scatter.20.cloned.1.call-done = f32[1280,256]{1,0:T(8,128)} async-done(((f32[1280,2048]{1,0:T(8,128)}), f32[1280,256]{1,0:T(8,128)}) %reduce-scatter.20.cloned.1.call-update) | async-done | bytes 1310736 | tf_op jit(solution)/shard_map/reduce_scatter | solution.py:225
  (248 shorter events, 267.5 us)
Async XLA Ops:
  7.2 65.5 %all-gather.15.cloned.1.call-start = ((), (), s32[]{:S(2)}) async-start(), calls=%async_computation.9 | async-start | bytes 2359296 | tf_op jit(solution)/shard_map/all_gather | solution.py:141
  9.2 76.6 %all-gather.11.cloned.1.call-start = ((), (), s32[]{:S(2)}) async-start(), calls=%async_computation.7 | async-start | bytes 2359296 | tf_op jit(solution)/shard_map/all_gather | solution.py:142
  11.1 100.8 %all-gather.13.cloned.1.call-start = ((), (), s32[]{:S(2)}) async-start(), calls=%async_computation.8 | async-start | bytes 2359296 | tf_op jit(solution)/shard_map/all_gather | solution.py:140
  11.9 172.5 %all-gather.17.cloned.1.call-start = ((), (), s32[]{:S(2)}) async-start(), calls=%async_computation.10 | async-start | bytes 2359296 | tf_op jit(solution)/shard_map/all_gather | solution.py:143
  12.7 251.0 %all-reduce.11.cloned.1.call-start = ((), (), s32[]{:S(2)}) async-start(), calls=%async_computation.11 | async-start | bytes 4194304 | tf_op jit(solution)/shard_map/psum | solution.py:193
  75.0 39.4 %collective-permute-start.6 = (bf16[256,512]{1,0:T(8,128)(2,1)S(1)}, bf16[256,512]{1,0:T(8,128)(2,1)S(1)}, u32[]{:S(2)}, u32[]{:S(2)}) collective-permute-start(bf16[256,512]{1,0:T(8,128)(2,1)S(1)} %convolution_convert_fusion.2), channel_id=1, source_target_pairs={{0,12},{4,16},{8,20},{12,24},{16,28},{1,13},{5,17},{9,21},{13,25},... | collective-permute-start | bytes 786440 | tf_op jit(solution)/shard_map/ppermute | solution.py:17
  78.5 37.2 %collective-permute-start.7 = (bf16[256,512]{1,0:T(8,128)(2,1)S(1)}, bf16[256,512]{1,0:T(8,128)(2,1)S(1)}, u32[]{:S(2)}, u32[]{:S(2)}) collective-permute-start(bf16[256,512]{1,0:T(8,128)(2,1)S(1)} %convolution_convert_fusion.2), channel_id=1, source_target_pairs={{0,8},{4,12},{8,16},{12,20},{16,24},{20,28},{1,9},{5,13},{9,17},{1... | collective-permute-start | bytes 786440 | tf_op jit(solution)/shard_map/ppermute | solution.py:17
  79.9 40.1 %collective-permute-start.8 = (bf16[256,512]{1,0:T(8,128)(2,1)S(1)}, bf16[256,512]{1,0:T(8,128)(2,1)S(1)}, u32[]{:S(2)}, u32[]{:S(2)}) collective-permute-start(bf16[256,512]{1,0:T(8,128)(2,1)S(1)} %convolution_convert_fusion.2), channel_id=1, source_target_pairs={{0,4},{4,8},{8,12},{12,16},{16,20},{20,24},{24,28},{1,5},{5,9},{9,... | collective-permute-start | bytes 786440 | tf_op jit(solution)/shard_map/ppermute | solution.py:17
  83.2 61.1 %collective-permute-start.9 = (bf16[256,512]{1,0:T(8,128)(2,1)S(1)}, bf16[256,512]{1,0:T(8,128)(2,1)S(1)}, u32[]{:S(2)}, u32[]{:S(2)}) collective-permute-start(bf16[256,512]{1,0:T(8,128)(2,1)S(1)} %convolution_convert_fusion.2), channel_id=1, source_target_pairs={{4,0},{8,4},{12,8},{16,12},{20,16},{24,20},{28,24},{5,1},{9,5},{13... | collective-permute-start | bytes 786440 | tf_op jit(solution)/shard_map/ppermute | solution.py:17
  84.5 61.5 %collective-permute-start.10 = (bf16[256,512]{1,0:T(8,128)(2,1)S(1)}, bf16[256,512]{1,0:T(8,128)(2,1)S(1)}, u32[]{:S(2)}, u32[]{:S(2)}) collective-permute-start(bf16[256,512]{1,0:T(8,128)(2,1)S(1)} %convolution_convert_fusion.2), channel_id=1, source_target_pairs={{8,0},{12,4},{16,8},{20,12},{24,16},{28,20},{9,1},{13,5},{17,9},{2... | collective-permute-start | bytes 786440 | tf_op jit(solution)/shard_map/ppermute | solution.py:17
  188.8 133.2 %all-gather.19.cloned.1.call-start = ((), (), s32[]{:S(2)}) async-start(), calls=%async_computation.12 | async-start | bytes 5898240 | tf_op jit(solution)/shard_map/all_gather | solution.py:188
  191.0 188.1 %all-gather.21.cloned.1.call-start = ((), (), s32[]{:S(2)}) async-start(), calls=%async_computation.13 | async-start | bytes 5898240 | tf_op jit(solution)/shard_map/all_gather | solution.py:189
  193.4 242.7 %all-gather.23.cloned.1.call-start = ((), (), s32[]{:S(2)}) async-start(), calls=%async_computation.14 | async-start | bytes 5898240 | tf_op jit(solution)/shard_map/all_gather | solution.py:190
  194.4 322.5 %all-reduce.15.cloned.1.call-start = ((), (), s32[]{:S(2)}) async-start(), calls=%async_computation.16 | async-start | bytes 4194304 | tf_op jit(solution)/shard_map/psum | solution.py:217
  448.9 124.1 %all-reduce.13.cloned.1.call-start = ((), (), s32[]{:S(2)}) async-start(), calls=%async_computation.15 | async-start | bytes 2097152 | tf_op jit(solution)/shard_map/psum | solution.py:202
  454.2 290.4 %all-reduce.17.cloned.1.call-start = ((), (), s32[]{:S(2)}) async-start(), calls=%async_computation.17 | async-start | bytes 4194304 | tf_op jit(solution)/shard_map/psum | solution.py:284
  618.5 31.8 %collective-permute-start.22 = (f32[256,512]{0,1:T(8,128)S(1)}, f32[256,512]{0,1:T(8,128)S(1)}, u32[]{:S(2)}, u32[]{:S(2)}) collective-permute-start(f32[256,512]{0,1:T(8,128)S(1)} %get-tuple-element.94), channel_id=1, source_target_pairs={{8,0},{12,4},{16,8},{20,12},{24,16},{28,20},{9,1},{13,5},{17,9},{2... | collective-permute-start | bytes 1572872 | tf_op jit(solution)/shard_map/ppermute | solution.py:17
  662.3 135.6 %reduce-scatter.8.cloned.1.call-start = ((), (), s32[]{:S(2)}) async-start(), calls=%async_computation.18 | async-start | bytes 4718592 | tf_op jit(solution)/shard_map/reduce_scatter | solution.py:288
  666.2 182.8 %reduce-scatter.14.cloned.1.call-start = ((), (), s32[]{:S(2)}) async-start(), calls=%async_computation.21 | async-start | bytes 4718592 | tf_op jit(solution)/shard_map/reduce_scatter | solution.py:291
  670.0 230.1 %reduce-scatter.10.cloned.1.call-start = ((), (), s32[]{:S(2)}) async-start(), calls=%async_computation.19 | async-start | bytes 4718592 | tf_op jit(solution)/shard_map/reduce_scatter | solution.py:289
  672.9 278.2 %reduce-scatter.12.cloned.1.call-start = ((), (), s32[]{:S(2)}) async-start(), calls=%async_computation.20 | async-start | bytes 4718592 | tf_op jit(solution)/shard_map/reduce_scatter | solution.py:290
  676.8 384.8 %reduce-scatter.16.cloned.1.call-start = ((), (), s32[]{:S(2)}) async-start(), calls=%async_computation.22 | async-start | bytes 11796480 | tf_op jit(solution)/shard_map/reduce_scatter | solution.py:223
  683.9 488.3 %reduce-scatter.18.cloned.1.call-start = ((), (), s32[]{:S(2)}) async-start(), calls=%async_computation.23 | async-start | bytes 11796480 | tf_op jit(solution)/shard_map/reduce_scatter | solution.py:224
  690.8 592.0 %reduce-scatter.20.cloned.1.call-start = ((), (), s32[]{:S(2)}) async-start(), calls=%async_computation.24 | async-start | bytes 11796480 | tf_op jit(solution)/shard_map/reduce_scatter | solution.py:225
  (51 other events, 874.4 us)
Sparse Core Ops, SparseCore 0:
  10.2 31.8 all-gather.14
  44.3 28.5 all-gather.10
  75.1 36.7 all-gather.12
  113.9 38.1 all-gather.16
  188.9 74.7 all-reduce.10
  265.9 56.0 all-gather.18
  324.3 54.8 all-gather.20
  380.8 55.2 all-gather.22
  449.0 67.8 all-reduce.14
  520.4 52.5 all-reduce.12
  662.5 82.0 all-reduce.16
  747.4 50.4 reduce-scatter.7
  800.9 48.0 reduce-scatter.13
  851.9 48.1 reduce-scatter.9
  902.9 48.1 reduce-scatter.11
  953.9 107.5 reduce-scatter.15
  1064.4 107.7 reduce-scatter.17
  1175.0 107.7 reduce-scatter.19
where the time goes:
time: 1300 us; the launch traced here: 1290 us
  waiting for transfers between devices  911 us (70%)
  matrix products  95.9 us (7%)
  local copies, waits for them, and re-layouts  86 us (7%)
  starting transfers between devices  79.2 us (6%)
  blocking collectives  68.4 us (5%)
  other arithmetic  32.5 us (2%)
  between operations  17.3 us (1%)
    reduce_scatter x1, waiting for transfers between devices, local(): lax.psum_scatter(d_down, 'fsdp', scatter_dimension=1, tiled=True)  111 us
    reduce_scatter x1, waiting for transfers between devices, local(): lax.psum_scatter(d_up_w, 'fsdp', scatter_dimension=0, tiled=True)  111 us
    reduce_scatter x1, waiting for transfers between devices, local(): lax.psum_scatter(d_gate_w, 'fsdp', scatter_dimension=0, tiled=True)  110 us
    ppermute x24, starting transfers between devices, shifted(): return lax.ppermute(block, axis, route)  78.2 us
    psum x1, waiting for transfers between devices, local(): lax.psum(contract_cols(d_gate_low, gate_full) + contract_cols(d_up_low, u...  62.4 us
    all_gather x1, waiting for transfers between devices, local(): lax.all_gather(w_gate.astype(low_type), 'fsdp', axis=0, tiled=True)  54.9 us
    psum x1, waiting for transfers between devices, local(): lax.psum(jnp.dot(hidden_act, down_full, preferred_element_type=jnp.float3...  53.9 us
    psum x1, waiting for transfers between devices, local(): lax.psum(jnp.dot(attended, out_full, preferred_element_type=jnp.float32),...  52.6 us
  transfers between devices with their start and end apart: 42, of which 22 were waited for; matrix products, arithmetic and copies ran while one was open for 13% of the time, Pallas kernels for 0%

commit v1 on v0

v1 whole, which is shorter than its diff:
```python
import functools

import jax
import jax.numpy as jnp
from jax import lax
from jax.experimental import pallas as pl
from jax.experimental.pallas import tpu as pltpu
from jax.sharding import Mesh, PartitionSpec as P

LOW = jnp.bfloat16
F32 = jnp.float32
CORES = 2
THRESHOLDS = (12, 16, 23, 32, 46, 64, 91)
EPSILON = 1e-06
MASKED = -1e30
SKEW = 128


def bucket_of(rel_offset):
    distance = jnp.abs(rel_offset)
    far_bucket = 8 + sum(((distance >= threshold).astype(jnp.int32) for threshold in THRESHOLDS))
    bucket_abs = jnp.where(distance < 8, distance, far_bucket)
    return bucket_abs + jnp.where(rel_offset > 0, 16, 0)


def bucket_onehot(buckets, seq_len):
    offset = lax.broadcasted_iota(jnp.int32, (buckets, 2 * seq_len), 1) - seq_len
    bucket = lax.broadcasted_iota(jnp.int32, (buckets, 2 * seq_len), 0)
    return bucket_of(offset) == bucket


def head_lanes(rows, width, head_width, head):
    lane = lax.broadcasted_iota(jnp.int32, (rows, width), 1)
    return (lane >= head * head_width) & (lane < (head + 1) * head_width)


def only(mask, values):
    return jnp.where(mask, values, jnp.zeros_like(values))


def block_place(block, core, near_count):
    return lax.rem(block, near_count) * CORES + lax.bitwise_xor(lax.div(block, near_count), core)


def bias_places(place_ref, step, blocks, rows, seq_len):
    core, near_count = place_ref[1], blocks // CORES
    query = block_place(step, core, near_count) * rows
    return [
        [
            pl.multiple_of(
                block_place(block, core, near_count) * rows - query - part * SKEW + seq_len - SKEW,
                SKEW,
            )
            for block in range(blocks)
        ]
        for part in range(rows // SKEW)
    ]


def forward_kernel(heads, rows, place_ref, qkv_ref, table_ref, o_ref, p_ref, skew_ref):
    step = pl.program_id(0)
    seq_len = qkv_ref.shape[0]
    width = qkv_ref.shape[1] // 3
    head_width = width // heads
    span = 2 * seq_len
    blocks = seq_len // rows

    @pl.when(step == 0)
    def _():
        one_hot = bucket_onehot(table_ref.shape[1], seq_len).astype(F32).astype(LOW)
        lines = jnp.dot(table_ref[...], one_hot, preferred_element_type=F32)
        for head in range(heads):
            line = jnp.broadcast_to(lines[head : head + 1], (SKEW, span))
            skew_ref[head] = pltpu.roll(line, span - SKEW, 1, stride=1, stride_axis=0)

    row = lax.broadcasted_iota(jnp.int32, (1, rows), 1)
    allowed = jnp.concatenate(
        [
            block_place(block, place_ref[1], blocks // CORES) * rows + row < place_ref[0]
            for block in range(blocks)
        ],
        1,
    )
    queries = qkv_ref[pl.ds(pl.multiple_of(step * rows, rows), rows), :width]
    keys = qkv_ref[:, width : 2 * width]
    values = qkv_ref[:, 2 * width :]
    total = jnp.zeros((rows, width), F32)
    places = bias_places(place_ref, step, blocks, rows, seq_len)
    for head in range(heads):
        scores = lax.dot_general(
            only(head_lanes(rows, width, head_width, head), queries),
            keys,
            (((1,), (1,)), ((), ())),
            preferred_element_type=F32,
        )
        bias = jnp.concatenate(
            [
                jnp.concatenate([skew_ref[head, :, pl.ds(place, rows)] for place in part], 1)
                for part in places
            ],
            0,
        )
        scores = jnp.where(allowed, scores + bias, MASKED)
        grown = jnp.exp(scores - jnp.max(scores, axis=1, keepdims=True))
        prob = (grown * (1.0 / jnp.sum(grown, axis=1, keepdims=True))).astype(LOW)
        p_ref[head] = prob
        total = total + jnp.dot(
            prob,
            only(head_lanes(seq_len, width, head_width, head), values),
            preferred_element_type=F32,
        )
    o_ref[...] = total.astype(LOW)


def attention_forward(qkv, table, place, heads, rows):
    seq_len, width = qkv.shape[0], qkv.shape[1] // 3
    return pl.pallas_call(
        functools.partial(forward_kernel, heads, rows),
        grid=(seq_len // rows,),
        in_specs=[
            pl.BlockSpec(memory_space=pltpu.SMEM),
            pl.BlockSpec(qkv.shape, lambda i: (0, 0)),
            pl.BlockSpec(table.shape, lambda i: (0, 0)),
        ],
        out_specs=[
            pl.BlockSpec((rows, width), lambda i: (i, 0)),
            pl.BlockSpec((heads, rows, seq_len), lambda i: (0, i, 0)),
        ],
        out_shape=[
            jax.ShapeDtypeStruct((seq_len, width), LOW),
            jax.ShapeDtypeStruct((heads, seq_len, seq_len), LOW),
        ],
        scratch_shapes=[pltpu.VMEM((heads, SKEW, 2 * seq_len), F32)],
        compiler_params=pltpu.CompilerParams(vmem_limit_bytes=32 * 2**20),
        cost_estimate=pl.CostEstimate(
            flops=4 * seq_len * seq_len * width * 4,
            bytes_accessed=2 * heads * seq_len * seq_len,
            transcendentals=heads * seq_len * seq_len,
        ),
        name="attention_forward",
    )(place, qkv, table)


def backward_kernel(
    heads, rows, place_ref, p_ref, do_ref, qkv_ref, d_ref, dt_ref, dk_sum, dv_sum, skew_ref
):
    step = pl.program_id(0)
    seq_len = qkv_ref.shape[0]
    width = qkv_ref.shape[1] // 3
    head_width = width // heads
    span = 2 * seq_len
    blocks = seq_len // rows

    @pl.when(step == 0)
    def _():
        dk_sum[...] = jnp.zeros_like(dk_sum)
        dv_sum[...] = jnp.zeros_like(dv_sum)
        skew_ref[...] = jnp.zeros_like(skew_ref)

    here = pl.ds(pl.multiple_of(step * rows, rows), rows)
    queries = qkv_ref[here, :width]
    keys = qkv_ref[:, width : 2 * width]
    values = qkv_ref[:, 2 * width :]
    grads = do_ref[...]
    total = jnp.zeros((rows, width), F32)
    places = bias_places(place_ref, step, blocks, rows, seq_len)
    for head in range(heads):
        own = head_lanes(rows, width, head_width, head)
        own_grads = only(own, grads)
        d_prob = lax.dot_general(
            own_grads, values, (((1,), (1,)), ((), ())), preferred_element_type=F32
        )
        prob_low = p_ref[head]
        prob = prob_low.astype(F32)
        weighed = prob * d_prob
        d_scores = (weighed - prob * jnp.sum(weighed, axis=1, keepdims=True)).astype(LOW)
        total = total + jnp.dot(
            d_scores,
            only(head_lanes(seq_len, width, head_width, head), keys),
            preferred_element_type=F32,
        )
        dk_sum[...] += lax.dot_general(
            d_scores, only(own, queries), (((0,), (0,)), ((), ())), preferred_element_type=F32
        )
        dv_sum[...] += lax.dot_general(
            prob_low, own_grads, (((0,), (0,)), ((), ())), preferred_element_type=F32
        )
        for part in range(rows // SKEW):
            for block in range(blocks):
                skew_ref[head, :, pl.ds(places[part][block], rows)] += d_scores[
                    part * SKEW : (part + 1) * SKEW, block * rows : (block + 1) * rows
                ].astype(F32)
    d_ref[here, :width] = total.astype(LOW)

    @pl.when(step == pl.num_programs(0) - 1)
    def _():
        d_ref[:, width : 2 * width] = dk_sum[...].astype(LOW)
        d_ref[:, 2 * width :] = dv_sum[...].astype(LOW)
        one_hot = bucket_onehot(dt_ref.shape[0], seq_len)
        row = lax.broadcasted_iota(jnp.int32, (SKEW, span), 0)
        column = lax.broadcasted_iota(jnp.int32, dt_ref.shape, 1)
        result = jnp.zeros(dt_ref.shape, F32)
        for head in range(heads):
            level = pltpu.roll(skew_ref[head], SKEW, 1)
            bit = 1
            while bit < SKEW:
                level = jnp.where((row & bit) != 0, pltpu.roll(level, span - bit, 1), level)
                bit *= 2
            line = jnp.sum(level, axis=0, keepdims=True)
            summed = jnp.sum(jnp.where(one_hot, line, 0.0), axis=1, keepdims=True)
            result = jnp.where(column == head, summed, result)
        dt_ref[...] = result


def attention_backward(prob, d_out, qkv, place, heads, rows, buckets):
    seq_len, width = d_out.shape
    return pl.pallas_call(
        functools.partial(backward_kernel, heads, rows),
        grid=(seq_len // rows,),
        in_specs=[
            pl.BlockSpec(memory_space=pltpu.SMEM),
            pl.BlockSpec((heads, rows, seq_len), lambda i: (0, i, 0)),
            pl.BlockSpec((rows, width), lambda i: (i, 0)),
            pl.BlockSpec(qkv.shape, lambda i: (0, 0)),
        ],
        out_specs=[
            pl.BlockSpec(qkv.shape, lambda i: (0, 0)),
            pl.BlockSpec((buckets, 128), lambda i: (0, 0)),
        ],
        out_shape=[
            jax.ShapeDtypeStruct(qkv.shape, LOW),
            jax.ShapeDtypeStruct((buckets, 128), F32),
        ],
        scratch_shapes=[
            pltpu.VMEM((seq_len, width), F32),
            pltpu.VMEM((seq_len, width), F32),
            pltpu.VMEM((heads, SKEW, 2 * seq_len), F32),
        ],
        compiler_params=pltpu.CompilerParams(vmem_limit_bytes=40 * 2**20),
        cost_estimate=pl.CostEstimate(
            flops=8 * seq_len * seq_len * width * 4,
            bytes_accessed=2 * heads * seq_len * seq_len,
            transcendentals=0,
        ),
        name="attention_backward",
    )(place, prob, d_out, qkv)


COLUMN = ("seq", "near", "core")
EXTRA = 8


def exchange(blocks, axes):
    return lax.all_to_all(blocks, axes, split_axis=0, concat_axis=0, tiled=True)


def swap(block, axis):
    return lax.ppermute(block, axis, [(0, 1), (1, 0)])


def after(value, *done):
    return lax.optimization_barrier((value,) + done)[0]


def rows_dot(left, right):
    return jnp.dot(left, right, preferred_element_type=F32)


def contract_cols(left, right):
    return lax.dot_general(left, right, (((1,), (1,)), ((), ())), preferred_element_type=F32)


def contract_rows(left, right):
    return lax.dot_general(left, right, (((0,), (0,)), ((), ())), preferred_element_type=F32)


def rms(values):
    return lax.rsqrt(jnp.mean(values * values, axis=1, keepdims=True) + EPSILON)


def norm_grad(inner, normed, inverse):
    return inverse * (inner - normed * jnp.mean(inner * normed, axis=1, keepdims=True))


def gelu_tanh(values):
    return jax.nn.gelu(values, approximate=True)


def local(
    inputs,
    cotangent,
    lengths,
    attn_scale,
    w_query,
    w_key,
    w_value,
    w_out,
    rel_table,
    ffn_scale,
    w_gate,
    w_up,
    w_down,
):
    seqs = lax.axis_size("seq")
    near_count = lax.axis_size("near")
    mp_count = lax.axis_size("mp")
    members = near_count * CORES
    sources = seqs * members
    tok_rows, model = inputs.shape
    seq_len = tok_rows * members
    own_rows = tok_rows // mp_count
    half_rows = seq_len // CORES
    shard = attn_scale.shape[0]
    table_rows, heads_mp = rel_table.shape
    buckets = table_rows * sources
    heads = heads_mp // members
    width = w_query.shape[1] // members
    hidden_width = w_gate.shape[1] // members

    near_at = lax.axis_index("near")
    core_at = lax.axis_index("core")
    mp_at = lax.axis_index("mp")
    member_at = near_at * CORES + core_at
    length = lax.dynamic_slice_in_dim(lengths, lax.axis_index("seq"), 1, 0)
    place = jnp.concatenate([length, jnp.reshape(core_at, (1,)).astype(jnp.int32)])

    def to_column(parts):
        return exchange(
            jnp.broadcast_to(parts[None], (seqs,) + parts.shape).reshape(
                (sources,) + parts.shape[1:]
            ),
            COLUMN,
        )

    def by_member(weight):
        return weight.reshape(weight.shape[0], members, -1)

    def scaled(weight, gain):
        low = weight.astype(LOW).astype(F32)
        return (low * gain.astype(LOW).astype(F32)[:, None]).astype(LOW)

    def over_mp(own, axis):
        shape = own.shape[:axis] + (mp_count,) + own.shape[axis:]
        blocks = lax.dynamic_update_index_in_dim(jnp.zeros(shape, own.dtype), own, mp_at, axis)
        moved = [(away, shifted(own, away)) for away in reversed(range(1, mp_count))]
        for away, block in moved:
            blocks = lax.dynamic_update_index_in_dim(blocks, block, mp_at ^ away, axis)
        return blocks

    def shifted(block, away):
        return lax.ppermute(block, "mp", [(i, i ^ away) for i in range(mp_count)])

    def in_near_order(own, moved):
        return jnp.stack(
            [jnp.where(near_at == 0, own, moved), jnp.where(near_at == 0, moved, own)], 0
        )

    def near_block_rows(block):
        own = lax.dynamic_slice_in_dim(block, mp_at * own_rows, own_rows, 0)
        moved = over_mp(swap(own, "near"), 0).reshape(tok_rows, model)
        return in_near_order(block, moved).reshape(half_rows, model)

    def gather_rows(own):
        near = in_near_order(own, swap(own, "near"))
        mine = over_mp(near, 1).reshape(half_rows, model)
        return mine, swap(mine, "core")

    def sum_cores(mine, other):
        arrived = swap(other.astype(LOW), "core")
        return (mine + arrived.astype(F32)).astype(LOW)

    def sum_mp(rows):
        pieces = rows.reshape(near_count, mp_count, own_rows, model)
        moved = []
        for away in reversed(range(1, mp_count)):
            piece = lax.dynamic_index_in_dim(pieces, mp_at ^ away, 1, keepdims=False)
            moved.append(shifted(piece, away))
        kept = lax.dynamic_index_in_dim(pieces, mp_at, 1, keepdims=False)
        return sum((piece.astype(F32) for piece in moved), kept.astype(F32))

    def sum_near(pair):
        sent = jnp.where(near_at == 0, pair[1], pair[0]).astype(LOW)
        kept = jnp.where(near_at == 0, pair[0], pair[1])
        return kept + swap(sent, "near").astype(F32)

    attn_parts = jnp.moveaxis(
        jnp.concatenate(
            [
                by_member(scaled(w_query, attn_scale)),
                by_member(scaled(w_key, attn_scale)),
                by_member(scaled(w_value, attn_scale)),
                by_member(w_out.T.astype(LOW)),
            ],
            2,
        ),
        1,
        0,
    )
    table_parts = rel_table.astype(LOW).reshape(table_rows, members, heads)
    table_parts = jnp.moveaxis(table_parts, 1, 0).reshape(members, 1, table_rows * heads)
    table_parts = jnp.pad(
        table_parts, ((0, 0), (0, EXTRA - 1), (0, 4 * width - table_rows * heads))
    )
    gate_up_parts = jnp.moveaxis(
        jnp.concatenate(
            [by_member(scaled(w_gate, ffn_scale)), by_member(scaled(w_up, ffn_scale))], 2
        ),
        1,
        0,
    )
    down_parts = jnp.moveaxis(by_member(w_down.T.astype(LOW)), 1, 0)

    attn_got = to_column(jnp.concatenate([attn_parts, table_parts], 1))
    attn_weights = attn_got[:, :shard].reshape(model, 4 * width)
    qkv_weight = attn_weights[:, : 3 * width]
    out_weight_t = attn_weights[:, 3 * width :]
    table = attn_got[:, shard, : table_rows * heads].reshape(buckets, heads)
    table = jnp.pad(table.T, ((0, 8 - heads), (0, 0)))

    mine_inputs = near_block_rows(inputs)
    mine_values = mine_inputs.astype(F32)
    mine_normed = (mine_values * rms(mine_values)).astype(LOW)
    normed_rows = jnp.concatenate([mine_normed, swap(mine_normed, "core")], 0)
    row_valid = (member_at * tok_rows + lax.iota(jnp.int32, tok_rows) < length)[:, None]
    masked = after(jnp.where(row_valid, cotangent, jnp.zeros_like(cotangent)), mine_inputs)
    mine_grad = near_block_rows(masked)
    other_grad = swap(mine_grad, "core")

    normed_rows = after(normed_rows, gate_up_parts, down_parts)
    gate_up_weight = to_column(gate_up_parts).reshape(model, 2 * hidden_width)
    down_weight_t = to_column(down_parts).reshape(model, hidden_width)

    qkv = rows_dot(normed_rows, qkv_weight).astype(LOW)
    attended, prob = attention_forward(qkv, table, place, heads, tok_rows)
    attended = after(attended, mine_grad, other_grad)
    mixed = sum_near(
        sum_mp(
            sum_cores(
                contract_cols(attended[:half_rows], out_weight_t),
                contract_cols(attended[half_rows:], out_weight_t),
            )
        )
    )

    own_inputs = lax.dynamic_slice_in_dim(inputs, mp_at * own_rows, own_rows, 0).astype(F32)
    own_cotangent = lax.dynamic_slice_in_dim(cotangent, mp_at * own_rows, own_rows, 0)
    own_first = member_at * tok_rows + mp_at * own_rows
    own_valid = (own_first + lax.iota(jnp.int32, own_rows) < length)[:, None]
    after_attn = own_inputs + mixed
    inv_two = rms(after_attn)
    normed_two = after_attn * inv_two
    halves = gather_rows(after(normed_two.astype(LOW), gate_up_weight))

    acts, d_gate_ups, d_norms, ffn_outs = [], [], [], []
    for rows, grad in zip(halves, (mine_grad, other_grad)):
        gate_up = rows_dot(rows, gate_up_weight)
        gate_pre, up_pre = gate_up[:, :hidden_width], gate_up[:, hidden_width:]
        gelu_value, gelu_pull = jax.vjp(gelu_tanh, gate_pre)
        acts.append((gelu_value * up_pre).astype(LOW))
        d_hidden = rows_dot(grad, down_weight_t)
        (d_gate_pre,) = gelu_pull(d_hidden * up_pre)
        d_gate_ups.append(
            jnp.concatenate([d_gate_pre.astype(LOW), (d_hidden * gelu_value).astype(LOW)], 1)
        )
        d_norms.append(contract_cols(d_gate_ups[-1], gate_up_weight))
        ffn_outs.append(contract_cols(acts[-1], down_weight_t))
    inner_two = sum_near(sum_mp(sum_cores(*d_norms)))

    def to_owners(grad):
        return exchange(grad.astype(LOW), COLUMN)

    def of_owner(got):
        parts = got.reshape((seqs, members) + got.shape[1:]).astype(F32)
        return jnp.moveaxis(jnp.sum(parts, axis=0), 0, 1)

    def flat(parts):
        return parts.reshape(shard, -1)

    d_down = to_owners(
        (contract_rows(mine_grad, acts[0]) + contract_rows(other_grad, acts[1])).reshape(
            sources, shard, -1
        )
    )
    d_gate_up = to_owners(
        (
            contract_rows(halves[0], d_gate_ups[0]) + contract_rows(halves[1], d_gate_ups[1])
        ).reshape(sources, shard, -1)
    )

    grad_one = jnp.where(own_valid, own_cotangent.astype(F32), 0.0) + norm_grad(
        inner_two, normed_two, inv_two
    )
    mine_one, other_one = gather_rows(after(grad_one.astype(LOW), d_down))
    d_attended = jnp.concatenate(
        [rows_dot(mine_one, out_weight_t), rows_dot(other_one, out_weight_t)], 0
    ).astype(LOW)
    d_qkv, d_table = attention_backward(prob, d_attended, qkv, place, heads, tok_rows, buckets)
    inner_cores = sum_cores(
        contract_cols(d_qkv[:half_rows], qkv_weight), contract_cols(d_qkv[half_rows:], qkv_weight)
    )
    d_out = to_owners(
        (
            contract_rows(mine_one, attended[:half_rows])
            + contract_rows(other_one, attended[half_rows:])
        ).reshape(sources, shard, -1)
    )
    ffn_cores = after(sum_cores(*ffn_outs), mine_one)
    ffn_pair = sum_mp(ffn_cores)
    inner_one = sum_near(sum_mp(after(inner_cores, d_gate_up)))
    table_sent = d_table[:, :heads].astype(LOW).reshape(sources, 1, table_rows * heads)
    table_sent = jnp.pad(
        table_sent, ((0, 0), (0, EXTRA - 1), (0, 3 * width - table_rows * heads))
    )
    d_qkv_w = contract_rows(normed_rows, d_qkv).astype(LOW).reshape(sources, shard, -1)
    d_qkv_got = to_owners(jnp.concatenate([d_qkv_w, table_sent], 1))

    normed_one = own_inputs * rms(own_inputs)
    grad_input = grad_one + norm_grad(inner_one, normed_one, rms(own_inputs))
    d_inputs = over_mp(grad_input.astype(LOW), 0).reshape(tok_rows, model)
    after_ffn = after_attn + sum_near(ffn_pair)
    own_out = jnp.where(own_valid, after_ffn, 0.0).astype(LOW)
    layer_out = over_mp(own_out, 0).reshape(tok_rows, model)

    g_gate_up = of_owner(d_gate_up)
    g_gate, g_up = flat(g_gate_up[:, :, :hidden_width]), flat(g_gate_up[:, :, hidden_width:])
    got_qkv = of_owner(d_qkv_got)
    g_query, g_key, g_value = (
        flat(got_qkv[:shard, :, i * width : (i + 1) * width]) for i in range(3)
    )
    d_rel_table = got_qkv[shard, :, : table_rows * heads].reshape(members, table_rows, heads)
    d_rel_table = jnp.moveaxis(d_rel_table, 0, 1).reshape(table_rows, heads_mp)

    def gain_grad(pairs):
        return sum(jnp.sum(w.astype(LOW).astype(F32) * g, axis=1) for w, g in pairs)

    gains = jnp.stack(
        [
            gain_grad([(w_query, g_query), (w_key, g_key), (w_value, g_value)]),
            gain_grad([(w_gate, g_gate), (w_up, g_up)]),
        ]
    )
    gains = sum((shifted(gains, away) for away in range(1, mp_count)), gains)
    attn_gain = attn_scale.astype(LOW).astype(F32)[:, None]
    ffn_gain = ffn_scale.astype(LOW).astype(F32)[:, None]
    return (
        layer_out,
        d_inputs,
        gains[0],
        g_query * attn_gain,
        g_key * attn_gain,
        g_value * attn_gain,
        flat(of_owner(d_out)).T,
        d_rel_table,
        gains[1],
        g_gate * ffn_gain,
        g_up * ffn_gain,
        flat(of_owner(d_down)).T,
    )


def solution(mesh):
    fsdp, mp = mesh.shape["fsdp"], mesh.shape["mp"]

    def run(*args):
        seqs = args[2].shape[0]
        members = fsdp // seqs
        inner = Mesh(
            mesh.devices.reshape(seqs, members // CORES, CORES, mp), ("seq", "near", "core", "mp")
        )
        rows, columns, first = P(COLUMN, None), P("mp", COLUMN), P(COLUMN)
        both = P(COLUMN, "mp")
        in_specs = (
            rows, rows, P(), first, both, both, both, columns, both, first, both, both, columns,
        )
        out_specs = (
            rows, rows, first, both, both, both, columns, both, first, both, both, columns,
        )
        return jax.shard_map(
            local, mesh=inner, in_specs=in_specs, out_specs=out_specs, check_vma=False
        )(*args)

    return run
```

time: 1300 us -> 511 us (0.39)
  waiting for transfers between devices: 911 us -> 203 us
  blocking collectives: 68.4 us -> 0 us
  matrix products: 95.9 us -> 71.1 us
  Pallas kernels: 0 us -> 19.9 us
  local copies, waits for them, and re-layouts: 86 us -> 67.9 us
  between operations: 17.3 us -> 2.43 us
    reduce_scatter x7 -> x0, waiting for transfers between devices: 501 us -> none  [the longest x1 111 us: local(): lax.psum_scatter(d_down, 'fsdp', scatter_dimension=1, tiled=True)]
    all_gather x7 -> x0, waiting for transfers between devices: 182 us -> none  [the longest x1 54.9 us: local(): lax.all_gather(w_gate.astype(low_type), 'fsdp', axis=0, tiled=True)]
    psum x4 -> x0, waiting for transfers between devices: 180 us -> none  [the longest x1 62.4 us: local(): lax.psum(contract_cols(d_gate_low, gate_full) + contract_cols(d_up_low, u...]
    ppermute x24 -> x49, waiting for transfers between devices: 47.8 us -> 168 us  [the longest x33 120 us: shifted(): return lax.ppermute(block, 'mp', [(i, i ^ away) for i in range(mp_count)])]
    all_to_all x0 -> x7, starting transfers between devices: none -> 41.3 us  [exchange(): return lax.all_to_all(blocks, axes, split_axis=0, concat_axis=0, tiled=True)]
    all_gather x3 -> x0, blocking collectives: 38.3 us -> none  [the longest x1 16 us: local(): lax.all_gather(ffn_scale.astype(low_type), 'fsdp', axis=0, tiled=True)]
    all_to_all x0 -> x7, waiting for transfers between devices: none -> 35.7 us  [exchange(): return lax.all_to_all(blocks, axes, split_axis=0, concat_axis=0, tiled=True)]
    unnamed x1 -> x0, blocking collectives: 30.1 us -> none
  transfers between devices with their start and end apart: 42 -> 56, of which waited for: 22 -> 29; matrix products, arithmetic and copies ran while one was open for 13% -> 29% of each run, Pallas kernels for 0% -> 4%
where the time goes in v1:
time: 511 us; the launch traced here: 501 us
  waiting for transfers between devices  203 us (40%)
  starting transfers between devices  91.7 us (18%)
  matrix products  71.1 us (14%)
  local copies, waits for them, and re-layouts  67.9 us (13%)
  other arithmetic  44.4 us (9%)
  Pallas kernels  19.9 us (4%)
    ppermute x33, waiting for transfers between devices, shifted(): return lax.ppermute(block, 'mp', [(i, i ^ away) for i in range(mp_count)])  120 us
    ppermute x16, waiting for transfers between devices, swap(): return lax.ppermute(block, axis, [(0, 1), (1, 0)])  47.6 us
    all_to_all x7, starting transfers between devices, exchange(): return lax.all_to_all(blocks, axes, split_axis=0, concat_axis=0, tiled=True)  41.3 us
    ppermute x33, starting transfers between devices, shifted(): return lax.ppermute(block, 'mp', [(i, i ^ away) for i in range(mp_count)])  39.9 us
    all_to_all x7, waiting for transfers between devices, exchange(): return lax.all_to_all(blocks, axes, split_axis=0, concat_axis=0, tiled=True)  35.7 us
    dot_general x8, matrix products, contract_cols(): lax.dot_general(left, right, (((1,), (1,)), ((), ())), preferred_element_...  26.8 us
    unnamed x133, local copies, waits for them, and re-layouts  25.3 us
    dot_general x7, matrix products, contract_rows(): lax.dot_general(left, right, (((0,), (0,)), ((), ())), preferred_element_...  23.9 us
  transfers between devices with their start and end apart: 56, of which 29 were waited for; matrix products, arithmetic and copies ran while one was open for 29% of the time, Pallas kernels for 4%

profile of v1, /device:TPU:0, one launch (start us, length us, event | category | flops | bytes accessed | tf_op | source)
XLA Modules:
  0.0 500.6 jit_solution(3277155567154467438)
XLA Ops:
  16.2 5.3 %all-to-all-start = ((bf16[8,264,512]{2,1,0:T(8,128)(2,1)}), bf16[8,264,512]{2,1,0:T(8,128)(2,1)}, u32[]{:S(2)}, u32[]{:S(2)}) async-start(bf16[8,264,512]{2,1,0:T(8,128)(2,1)} %bitcast.25), calls=%async_computation | async-start | bytes 4325376 | tf_op jit(solution)/shard_map/all_to_all | solution.py:254
  42.7 5.5 %collective-permute-done.2 = bf16[64,2048]{1,0:T(8,128)(2,1)S(1)} collective-permute-done((bf16[64,2048]{1,0:T(8,128)(2,1)}, bf16[64,2048]{1,0:T(8,128)(2,1)S(1)}, u32[]{:S(2)}, u32[]{:S(2)}) %collective-permute-start.2) | collective-permute-done | bytes 262176 | tf_op jit(solution)/shard_map/ppermute | solution.py:351
  78.2 7.5 %attention_forward.1 = (bf16[1024,128]{1,0:T(8,128)(2,1)S(1)}, bf16[2,1024,1024]{2,1,0:T(8,128)(2,1)S(1)}) custom-call(s32[2]{0:T(128)S(1)} %pad_add_fusion.place_ref, bf16[1024,384]{1,0:T(8,128)(2,1)S(1)} %convolution_convert_fusion.5.qkv_ref, bf16[8,32]{1,0:T(8,128)(2,1)S(1)} %pad.13.table_ref), custom_call_target="tpu_custom_call" | custom-call | flops 2147483648 | bytes 4194304 | tf_op jit(solution)/shard_map/attention_forward/pallas_call | solution.py:117
  105.2 12.2 %collective-permute-done.11 = bf16[2,64,2048]{2,1,0:T(8,128)(2,1)S(1)} collective-permute-done((bf16[2,64,2048]{2,1,0:T(8,128)(2,1)S(1)}, bf16[2,64,2048]{2,1,0:T(8,128)(2,1)S(1)}, u32[]{:S(2)}, u32[]{:S(2)}) %collective-permute-start.11) | collective-permute-done | bytes 524320 | tf_op jit(solution)/shard_map/ppermute | solution.py:351
  117.4 10.8 %collective-permute-done.12 = bf16[2,64,2048]{2,1,0:T(8,128)(2,1)S(1)} collective-permute-done((bf16[2,64,2048]{2,1,0:T(8,128)(2,1)S(1)}, bf16[2,64,2048]{2,1,0:T(8,128)(2,1)S(1)}, u32[]{:S(2)}, u32[]{:S(2)}) %collective-permute-start.12) | collective-permute-done | bytes 524320 | tf_op jit(solution)/shard_map/ppermute | solution.py:351
  130.3 17.4 %collective-permute-done.14 = bf16[64,2048]{1,0:T(8,128)(2,1)S(1)} collective-permute-done((bf16[64,2048]{1,0:T(8,128)(2,1)S(1)}, bf16[64,2048]{1,0:T(8,128)(2,1)S(1)}, u32[]{:S(2)}, u32[]{:S(2)}) %collective-permute-start.14) | collective-permute-done | bytes 262176 | tf_op jit(solution)/shard_map/ppermute | solution.py:258
  148.9 10.4 %all-to-all-done.1 = bf16[8,256,640]{2,1,0:T(8,128)(2,1)} async-done(((bf16[8,256,640]{2,1,0:T(8,128)(2,1)}), bf16[8,256,640]{2,1,0:T(8,128)(2,1)}, u32[]{:S(2)}, u32[]{:S(2)}) %all-to-all-start.1) | async-done | bytes 2621472 | tf_op jit(solution)/shard_map/all_to_all | solution.py:254
  159.3 7.9 %collective-permute-done.15 = bf16[64,2048]{1,0:T(8,128)(2,1)S(1)} collective-permute-done((bf16[64,2048]{1,0:T(8,128)(2,1)S(1)}, bf16[64,2048]{1,0:T(8,128)(2,1)S(1)}, u32[]{:S(2)}, u32[]{:S(2)}) %collective-permute-start.15) | collective-permute-done | bytes 262176 | tf_op jit(solution)/shard_map/ppermute | solution.py:258
  177.3 5.9 %collective-permute-done.16 = bf16[2,64,2048]{2,1,0:T(8,128)(2,1)} collective-permute-done((bf16[2,64,2048]{2,1,0:T(8,128)(2,1)}, bf16[2,64,2048]{2,1,0:T(8,128)(2,1)}, u32[]{:S(2)}, u32[]{:S(2)}) %collective-permute-start.16) | collective-permute-done | bytes 524320 | tf_op jit(solution)/shard_map/ppermute | solution.py:351
  184.3 8.7 %collective-permute-done.17 = bf16[2,64,2048]{2,1,0:T(8,128)(2,1)S(1)} collective-permute-done((bf16[2,64,2048]{2,1,0:T(8,128)(2,1)}, bf16[2,64,2048]{2,1,0:T(8,128)(2,1)S(1)}, u32[]{:S(2)}, u32[]{:S(2)}) %collective-permute-start.17) | collective-permute-done | bytes 524320 | tf_op jit(solution)/shard_map/ppermute | solution.py:351
  193.3 14.8 %all-to-all-done.2 = bf16[8,256,320]{1,2,0:T(8,128)(2,1)} async-done(((bf16[8,256,320]{1,2,0:T(8,128)(2,1)}), bf16[8,256,320]{1,2,0:T(8,128)(2,1)}, u32[]{:S(2)}, u32[]{:S(2)}) %all-to-all-start.2) | async-done | bytes 1310752 | tf_op jit(solution)/shard_map/all_to_all | solution.py:254
  243.4 14.1 %all-to-all-start.3 = ((bf16[8,256,320]{1,2,0:T(8,128)(2,1)}), bf16[8,256,320]{1,2,0:T(8,128)(2,1)}, u32[]{:S(2)}, u32[]{:S(2)}) async-start(bf16[8,256,320]{1,2,0:T(8,128)(2,1)} %bitcast.304), calls=%async_computation.3 | async-start | bytes 2621440 | tf_op jit(solution)/shard_map/all_to_all | solution.py:254
  265.5 5.8 %fusion.57 = f32[2048,640]{1,0:T(8,128)} fusion(bf16[512,2048]{1,0:T(8,128)(2,1)} %collective-permute-done.19, bf16[512,320]{1,0:T(8,128)(2,1)S(1)} %copy-done.49, bf16[512,320]{1,0:T(8,128)(2,1)S(1)} %get-tuple-element.105), kind=kOutput, calls=%fused_computation.158 | convolution fusion | flops 1343488000 | bytes 7995392 | tf_op jit(solution)/shard_map/dot_general | solution.py:274
  271.3 13.8 %collective-permute-done.25 = bf16[64,2048]{1,0:T(8,128)(2,1)S(1)} collective-permute-done((bf16[64,2048]{1,0:T(8,128)(2,1)S(1)}, bf16[64,2048]{1,0:T(8,128)(2,1)S(1)}, u32[]{:S(2)}, u32[]{:S(2)}) %collective-permute-start.25) | collective-permute-done | bytes 262176 | tf_op jit(solution)/shard_map/ppermute | solution.py:258
  289.8 6.1 %add_convert_fusion = bf16[2048,640]{1,0:T(8,128)(2,1)} fusion(f32[2048,640]{1,0:T(8,128)} %fusion.57, bf16[512,2048]{1,0:T(8,128)(2,1)S(1)} %bitcast.285, bf16[512,320]{1,0:T(8,128)(2,1)} %copy-done.52, bf16[512,320]{1,0:T(8,128)(2,1)} %copy-done.51), kind=kOutput, calls=%fused_computation.1 | convolution fusion | flops 1346109440 | bytes 10616832 | tf_op jit(solution)/shard_map/dot_general | solution.py:274
  308.6 8.9 %collective-permute-done.27 = bf16[2,64,2048]{2,1,0:T(8,128)(2,1)S(1)} collective-permute-done((bf16[2,64,2048]{2,1,0:T(8,128)(2,1)S(1)}, bf16[2,64,2048]{2,1,0:T(8,128)(2,1)S(1)}, u32[]{:S(2)}, u32[]{:S(2)}) %collective-permute-start.27) | collective-permute-done | bytes 524320 | tf_op jit(solution)/shard_map/ppermute | solution.py:351
  317.6 10.7 %collective-permute-done.28 = bf16[2,64,2048]{2,1,0:T(8,128)(2,1)S(1)} collective-permute-done((bf16[2,64,2048]{2,1,0:T(8,128)(2,1)S(1)}, bf16[2,64,2048]{2,1,0:T(8,128)(2,1)S(1)}, u32[]{:S(2)}, u32[]{:S(2)}) %collective-permute-start.28) | collective-permute-done | bytes 524320 | tf_op jit(solution)/shard_map/ppermute | solution.py:351
  336.0 8.4 %collective-permute-done.30 = bf16[2,64,2048]{2,1,0:T(8,128)(2,1)S(1)} collective-permute-done((bf16[2,64,2048]{2,1,0:T(8,128)(2,1)S(1)}, bf16[2,64,2048]{2,1,0:T(8,128)(2,1)S(1)}, u32[]{:S(2)}, u32[]{:S(2)}) %collective-permute-start.30) | collective-permute-done | bytes 524320 | tf_op jit(solution)/shard_map/ppermute | solution.py:351
  344.4 9.7 %collective-permute-done.31 = bf16[2,64,2048]{2,1,0:T(8,128)(2,1)S(1)} collective-permute-done((bf16[2,64,2048]{2,1,0:T(8,128)(2,1)S(1)}, bf16[2,64,2048]{2,1,0:T(8,128)(2,1)S(1)}, u32[]{:S(2)}, u32[]{:S(2)}) %collective-permute-start.31) | collective-permute-done | bytes 524320 | tf_op jit(solution)/shard_map/ppermute | solution.py:351
  358.0 8.5 %collective-permute-done.33 = bf16[64,2048]{1,0:T(8,128)(2,1)S(1)} collective-permute-done((bf16[64,2048]{1,0:T(8,128)(2,1)S(1)}, bf16[64,2048]{1,0:T(8,128)(2,1)S(1)}, u32[]{:S(2)}, u32[]{:S(2)}) %collective-permute-start.33) | collective-permute-done | bytes 262176 | tf_op jit(solution)/shard_map/ppermute | solution.py:258
  387.1 12.4 %attention_backward.1 = (bf16[1024,384]{1,0:T(8,128)(2,1)S(1)}, f32[32,128]{1,0:T(8,128)S(1)}) custom-call(s32[2]{0:T(128)S(1)} %pad_add_fusion.place_ref, bf16[2,1024,1024]{2,1,0:T(8,128)(2,1)S(1)} %copy-done.1, bf16[1024,128]{1,0:T(8,128)(2,1)S(1)} %pad_maximum_fusion.13.do_ref, bf16[1024,384]{1,0:T(8,128)(2,1)S(1)} %convolution_convert_fusion.5.qkv_ref), custom_call_target="tpu_custom_call" | custom-call | flops 4294967296 | bytes 4194304 | tf_op jit(solution)/shard_map/attention_backward/pallas_call | solution.py:217
  444.2 8.4 %collective-permute-done.39 = bf16[2,64,2048]{2,1,0:T(8,128)(2,1)} collective-permute-done((bf16[2,64,2048]{2,1,0:T(8,128)(2,1)}, bf16[2,64,2048]{2,1,0:T(8,128)(2,1)}, u32[]{:S(2)}, u32[]{:S(2)}) %collective-permute-start.39) | collective-permute-done | bytes 524320 | tf_op jit(solution)/shard_map/ppermute | solution.py:351
  452.6 10.1 %collective-permute-done.40 = bf16[2,64,2048]{2,1,0:T(8,128)(2,1)} collective-permute-done((bf16[2,64,2048]{2,1,0:T(8,128)(2,1)}, bf16[2,64,2048]{2,1,0:T(8,128)(2,1)}, u32[]{:S(2)}, u32[]{:S(2)}) %collective-permute-start.40) | collective-permute-done | bytes 524320 | tf_op jit(solution)/shard_map/ppermute | solution.py:351
  489.9 6.1 %collective-permute-done.43 = bf16[64,2048]{1,0:T(8,128)(2,1)S(1)} collective-permute-done((bf16[64,2048]{1,0:T(8,128)(2,1)S(1)}, bf16[64,2048]{1,0:T(8,128)(2,1)S(1)}, u32[]{:S(2)}, u32[]{:S(2)}) %collective-permute-start.43) | collective-permute-done | bytes 262176 | tf_op jit(solution)/shard_map/ppermute | solution.py:351
  (363 shorter events, 269.0 us)
Async XLA Ops:
  16.2 55.9 %all-to-all-start = ((bf16[8,264,512]{2,1,0:T(8,128)(2,1)}), bf16[8,264,512]{2,1,0:T(8,128)(2,1)}, u32[]{:S(2)}, u32[]{:S(2)}) async-start(bf16[8,264,512]{2,1,0:T(8,128)(2,1)} %bitcast.25), calls=%async_computation | async-start | bytes 4325376 | tf_op jit(solution)/shard_map/all_to_all | solution.py:254
  26.0 22.2 %collective-permute-start.2 = (bf16[64,2048]{1,0:T(8,128)(2,1)}, bf16[64,2048]{1,0:T(8,128)(2,1)S(1)}, u32[]{:S(2)}, u32[]{:S(2)}) collective-permute-start(bf16[64,2048]{1,0:T(8,128)(2,1)} %collective-permute-done), channel_id=1, source_target_pairs={{0,2},{1,3},{2,0},{3,1},{4,6},{5,7},{6,4},{7,5},{8,10},{9,11},{10,... | collective-permute-start | bytes 786440 | tf_op jit(solution)/shard_map/ppermute | solution.py:351
  59.8 27.9 %collective-permute-start.9 = (bf16[512,2048]{1,0:T(8,128)(2,1)S(1)}, bf16[512,2048]{1,0:T(8,128)(2,1)}, u32[]{:S(2)}, u32[]{:S(2)}) collective-permute-start(bf16[512,2048]{1,0:T(8,128)(2,1)S(1)} %bitcast.286), channel_id=1, source_target_pairs={{0,4},{4,0},{1,5},{5,1},{2,6},{6,2},{3,7},{7,3},{8,12},{12,8},{9,1... | collective-permute-start | bytes 6291464 | tf_op jit(solution)/shard_map/ppermute | solution.py:258
  94.3 65.0 %all-to-all-start.1 = ((bf16[8,256,640]{2,1,0:T(8,128)(2,1)}), bf16[8,256,640]{2,1,0:T(8,128)(2,1)}, u32[]{:S(2)}, u32[]{:S(2)}) async-start(bf16[8,256,640]{2,1,0:T(8,128)(2,1)} %bitcast.291), calls=%async_computation.1 | async-start | bytes 5242880 | tf_op jit(solution)/shard_map/all_to_all | solution.py:254
  104.2 24.0 %collective-permute-start.12 = (bf16[2,64,2048]{2,1,0:T(8,128)(2,1)S(1)}, bf16[2,64,2048]{2,1,0:T(8,128)(2,1)S(1)}, u32[]{:S(2)}, u32[]{:S(2)}) collective-permute-start(bf16[2,64,2048]{2,1,0:T(8,128)(2,1)S(1)} %get-tuple-element.109), channel_id=1, source_target_pairs={{0,2},{1,3},{2,0},{3,1},{4,6},{5,7},{6,4},{7,5},{8,10},{9,11},{10,... | collective-permute-start | bytes 1572872 | tf_op jit(solution)/shard_map/ppermute | solution.py:351
  104.7 23.6 %collective-permute-start.13 = (bf16[2,64,2048]{2,1,0:T(8,128)(2,1)S(1)}, bf16[2,64,2048]{2,1,0:T(8,128)(2,1)S(1)}, u32[]{:S(2)}, u32[]{:S(2)}) collective-permute-start(bf16[2,64,2048]{2,1,0:T(8,128)(2,1)S(1)} %get-tuple-element.108), channel_id=1, source_target_pairs={{0,1},{1,0},{2,3},{3,2},{4,5},{5,4},{6,7},{7,6},{8,9},{9,8},{10,11... | collective-permute-start | bytes 1572872 | tf_op jit(solution)/shard_map/ppermute | solution.py:351
  171.6 36.5 %all-to-all-start.2 = ((bf16[8,256,320]{1,2,0:T(8,128)(2,1)}), bf16[8,256,320]{1,2,0:T(8,128)(2,1)}, u32[]{:S(2)}, u32[]{:S(2)}) async-start(bf16[8,256,320]{1,2,0:T(8,128)(2,1)} %bitcast.57), calls=%async_computation.2 | async-start | bytes 2621440 | tf_op jit(solution)/shard_map/all_to_all | solution.py:254
  236.3 25.5 %collective-permute-start.22 = (bf16[2,64,2048]{2,1,0:T(8,128)(2,1)}, bf16[2,64,2048]{2,1,0:T(8,128)(2,1)}, u32[]{:S(2)}, u32[]{:S(2)}) collective-permute-start(bf16[2,64,2048]{2,1,0:T(8,128)(2,1)} %get-tuple-element.100), channel_id=1, source_target_pairs={{0,3},{1,2},{2,1},{3,0},{4,7},{5,6},{6,5},{7,4},{8,11},{9,10},{10,... | collective-permute-start | bytes 1572872 | tf_op jit(solution)/shard_map/ppermute | solution.py:351
  236.7 25.6 %collective-permute-start.23 = (bf16[2,64,2048]{2,1,0:T(8,128)(2,1)}, bf16[2,64,2048]{2,1,0:T(8,128)(2,1)}, u32[]{:S(2)}, u32[]{:S(2)}) collective-permute-start(bf16[2,64,2048]{2,1,0:T(8,128)(2,1)} %get-tuple-element.102), channel_id=1, source_target_pairs={{0,2},{1,3},{2,0},{3,1},{4,6},{5,7},{6,4},{7,5},{8,10},{9,11},{10,... | collective-permute-start | bytes 1572872 | tf_op jit(solution)/shard_map/ppermute | solution.py:351
  238.3 24.1 %collective-permute-start.24 = (bf16[2,64,2048]{2,1,0:T(8,128)(2,1)}, bf16[2,64,2048]{2,1,0:T(8,128)(2,1)}, u32[]{:S(2)}, u32[]{:S(2)}) collective-permute-start(bf16[2,64,2048]{2,1,0:T(8,128)(2,1)} %get-tuple-element.101), channel_id=1, source_target_pairs={{0,1},{1,0},{2,3},{3,2},{4,5},{5,4},{6,7},{7,6},{8,9},{9,8},{10,11... | collective-permute-start | bytes 1572872 | tf_op jit(solution)/shard_map/ppermute | solution.py:351
  243.4 46.1 %all-to-all-start.3 = ((bf16[8,256,320]{1,2,0:T(8,128)(2,1)}), bf16[8,256,320]{1,2,0:T(8,128)(2,1)}, u32[]{:S(2)}, u32[]{:S(2)}) async-start(bf16[8,256,320]{1,2,0:T(8,128)(2,1)} %bitcast.304), calls=%async_computation.3 | async-start | bytes 2621440 | tf_op jit(solution)/shard_map/all_to_all | solution.py:254
  261.6 40.8 %collective-permute-start.20 = (bf16[512,2048]{1,0:T(8,128)(2,1)}, bf16[512,2048]{1,0:T(8,128)(2,1)}, u32[]{:S(2)}, u32[]{:S(2)}) collective-permute-start(bf16[512,2048]{1,0:T(8,128)(2,1)} %convolution_convert_fusion.2), channel_id=1, source_target_pairs={{0,4},{4,0},{1,5},{5,1},{2,6},{6,2},{3,7},{7,3},{8,12},{12,8},{9,1... | collective-permute-start | bytes 6291464 | tf_op jit(solution)/shard_map/ppermute | solution.py:258
  295.9 76.1 %all-to-all-start.4 = ((bf16[8,256,640]{2,1,0:T(8,128)(2,1)}), bf16[8,256,640]{2,1,0:T(8,128)(2,1)}, u32[]{:S(2)}, u32[]{:S(2)}) async-start(bf16[8,256,640]{2,1,0:T(8,128)(2,1)} %bitcast.282), calls=%async_computation.4 | async-start | bytes 5242880 | tf_op jit(solution)/shard_map/all_to_all | solution.py:254
  305.2 23.1 %collective-permute-start.28 = (bf16[2,64,2048]{2,1,0:T(8,128)(2,1)S(1)}, bf16[2,64,2048]{2,1,0:T(8,128)(2,1)S(1)}, u32[]{:S(2)}, u32[]{:S(2)}) collective-permute-start(bf16[2,64,2048]{2,1,0:T(8,128)(2,1)S(1)} %pad_maximum_fusion.6), channel_id=1, source_target_pairs={{0,2},{1,3},{2,0},{3,1},{4,6},{5,7},{6,4},{7,5},{8,10},{9,11},{10,... | collective-permute-start | bytes 1572872 | tf_op jit(solution)/shard_map/ppermute | solution.py:351
  329.2 24.9 %collective-permute-start.31 = (bf16[2,64,2048]{2,1,0:T(8,128)(2,1)S(1)}, bf16[2,64,2048]{2,1,0:T(8,128)(2,1)S(1)}, u32[]{:S(2)}, u32[]{:S(2)}) collective-permute-start(bf16[2,64,2048]{2,1,0:T(8,128)(2,1)S(1)} %get-tuple-element.99), channel_id=1, source_target_pairs={{0,2},{1,3},{2,0},{3,1},{4,6},{5,7},{6,4},{7,5},{8,10},{9,11},{10,... | collective-permute-start | bytes 1572872 | tf_op jit(solution)/shard_map/ppermute | solution.py:351
  330.7 23.4 %collective-permute-start.32 = (bf16[2,64,2048]{2,1,0:T(8,128)(2,1)S(1)}, bf16[2,64,2048]{2,1,0:T(8,128)(2,1)S(1)}, u32[]{:S(2)}, u32[]{:S(2)}) collective-permute-start(bf16[2,64,2048]{2,1,0:T(8,128)(2,1)S(1)} %get-tuple-element.98), channel_id=1, source_target_pairs={{0,1},{1,0},{2,3},{3,2},{4,5},{5,4},{6,7},{7,6},{8,9},{9,8},{10,11... | collective-permute-start | bytes 1572872 | tf_op jit(solution)/shard_map/ppermute | solution.py:351
  336.0 46.5 %collective-permute-start.37 = (bf16[512,2048]{1,0:T(8,128)(2,1)S(1)}, bf16[512,2048]{1,0:T(8,128)(2,1)}, u32[]{:S(2)}, u32[]{:S(2)}) collective-permute-start(bf16[512,2048]{1,0:T(8,128)(2,1)S(1)} %bitcast.298), channel_id=1, source_target_pairs={{0,4},{4,0},{1,5},{5,1},{2,6},{6,2},{3,7},{7,3},{8,12},{12,8},{9,1... | collective-permute-start | bytes 6291464 | tf_op jit(solution)/shard_map/ppermute | solution.py:258
  368.5 61.4 %collective-permute-start.34 = (bf16[64,2048]{1,0:T(8,128)(2,1)}, bf16[64,2048]{1,0:T(8,128)(2,1)}, u32[]{:S(2)}, u32[]{:S(2)}) collective-permute-start(bf16[64,2048]{1,0:T(8,128)(2,1)} %get-tuple-element.87), channel_id=1, source_target_pairs={{0,3},{1,2},{2,1},{3,0},{4,7},{5,6},{6,5},{7,4},{8,11},{9,10},{10,... | collective-permute-start | bytes 786440 | tf_op jit(solution)/shard_map/ppermute | solution.py:351
  369.0 61.9 %collective-permute-start.35 = (bf16[64,2048]{1,0:T(8,128)(2,1)}, bf16[64,2048]{1,0:T(8,128)(2,1)}, u32[]{:S(2)}, u32[]{:S(2)}) collective-permute-start(bf16[64,2048]{1,0:T(8,128)(2,1)} %get-tuple-element.87), channel_id=1, source_target_pairs={{0,2},{1,3},{2,0},{3,1},{4,6},{5,7},{6,4},{7,5},{8,10},{9,11},{10,... | collective-permute-start | bytes 786440 | tf_op jit(solution)/shard_map/ppermute | solution.py:351
  370.5 69.6 %collective-permute-start.36 = (bf16[64,2048]{1,0:T(8,128)(2,1)}, bf16[64,2048]{1,0:T(8,128)(2,1)}, u32[]{:S(2)}, u32[]{:S(2)}) collective-permute-start(bf16[64,2048]{1,0:T(8,128)(2,1)} %get-tuple-element.87), channel_id=1, source_target_pairs={{0,1},{1,0},{2,3},{3,2},{4,5},{5,4},{6,7},{7,6},{8,9},{9,8},{10,11... | collective-permute-start | bytes 786440 | tf_op jit(solution)/shard_map/ppermute | solution.py:351
  402.3 29.6 %collective-permute-start.38 = (bf16[512,2048]{1,0:T(8,128)(2,1)}, bf16[512,2048]{1,0:T(8,128)(2,1)}, u32[]{:S(2)}, u32[]{:S(2)}) collective-permute-start(bf16[512,2048]{1,0:T(8,128)(2,1)} %convolution_convert_fusion.1), channel_id=1, source_target_pairs={{0,4},{4,0},{1,5},{5,1},{2,6},{6,2},{3,7},{7,3},{8,12},{12,8},{9,1... | collective-permute-start | bytes 6291464 | tf_op jit(solution)/shard_map/ppermute | solution.py:258
  425.9 43.0 %all-to-all-start.5 = ((bf16[8,264,384]{2,1,0:T(8,128)(2,1)}), bf16[8,264,384]{2,1,0:T(8,128)(2,1)S(1)}, u32[]{:S(2)}, u32[]{:S(2)}) async-start(bf16[8,264,384]{2,1,0:T(8,128)(2,1)} %fusion.4), calls=%async_computation.5 | async-start | bytes 3244032 | tf_op jit(solution)/shard_map/all_to_all | solution.py:254
  437.1 25.6 %collective-permute-start.40 = (bf16[2,64,2048]{2,1,0:T(8,128)(2,1)}, bf16[2,64,2048]{2,1,0:T(8,128)(2,1)}, u32[]{:S(2)}, u32[]{:S(2)}) collective-permute-start(bf16[2,64,2048]{2,1,0:T(8,128)(2,1)} %get-tuple-element.96), channel_id=1, source_target_pairs={{0,2},{1,3},{2,0},{3,1},{4,6},{5,7},{6,4},{7,5},{8,10},{9,11},{10,... | collective-permute-start | bytes 1572872 | tf_op jit(solution)/shard_map/ppermute | solution.py:351
  438.6 24.1 %collective-permute-start.41 = (bf16[2,64,2048]{2,1,0:T(8,128)(2,1)S(1)}, bf16[2,64,2048]{2,1,0:T(8,128)(2,1)}, u32[]{:S(2)}, u32[]{:S(2)}) collective-permute-start(bf16[2,64,2048]{2,1,0:T(8,128)(2,1)S(1)} %get-tuple-element.95), channel_id=1, source_target_pairs={{0,1},{1,0},{2,3},{3,2},{4,5},{5,4},{6,7},{7,6},{8,9},{9,8},{10,11... | collective-permute-start | bytes 1572872 | tf_op jit(solution)/shard_map/ppermute | solution.py:351
  (91 other events, 953.4 us)
